TPU v7x, 32 devices: a whole 2x2x4 slice. The times are simulated.
32 devices in a mesh: dp: 8 (over z, y), tensor: 4 (over x, core).
Axes of the slice: x: 2, y: 2, z: 4, core: 2. Of those that a mesh axis runs over, the one named last changes fastest.
Arguments:
- gate_pre: bfloat16 [32, 64, 28672], P('dp', None, 'tensor'), may hold values from -6 to 6
- up_pre: bfloat16 [32, 64, 28672], P('dp', None, 'tensor'), may hold values from -6 to 6
- out_grad: bfloat16 [32, 64, 8192], P('dp', None, 'tensor'), may hold values from -60 to 60
- lengths: int32 [32], P('dp'), may hold values from 1 to 64, 1280 in all
- proj_hidden: bfloat16 [28672, 64], P('tensor'), may hold values from -0.03125 to 0.03125
- proj_out: bfloat16 [8192, 64], P('tensor'), may hold values from -0.0625 to 0.0625
- query_grads: float32 [64, 4096], P('dp'), may hold values from -6 to 6
Outputs:
- scores: float32 [32, 64], P('dp')
Inputs may be any that keep to these rules, and one draw needn't show every extreme that they name: `lengths`: each example has 1 to 64 live tokens, and some example has exactly 64.
All inputs are finite; a program needn't handle non-finite values. No bound on the sum of `lengths` on one device may be relied on, other than what follows from the above.
Results may differ from a plain program's by a relative error of at most 0.003.
Values sent between devices are 32-bit elements; how exact they have to be, the bound alone decides.
A program may use at most 64 MiB of HBM per device.

v0:
```python
import jax
import jax.numpy as jnp
from jax import lax
from jax.sharding import PartitionSpec as P


def per_device(gate_pre, up_pre, out_grad, lengths, proj_hidden, proj_out, query_grads):
    e_dev = gate_pre.shape[0]
    seq_len = gate_pre.shape[1]
    rank = proj_hidden.shape[1]
    hidden = (jax.nn.silu(gate_pre.astype(jnp.float32)) * up_pre.astype(jnp.float32)).astype(
        jnp.bfloat16
    )
    in_part = jnp.einsum("esf,fr->esr", hidden, proj_hidden, preferred_element_type=jnp.float32)
    out_part = jnp.einsum("esd,dr->esr", out_grad, proj_out, preferred_element_type=jnp.float32)
    joined = lax.psum(jnp.concatenate([in_part, out_part], axis=2), "tensor")
    live = (jnp.arange(seq_len, dtype=jnp.int32)[None, :] < lengths[:, None]).astype(jnp.float32)
    in_proj = joined[:, :, :rank] * live[:, :, None]
    out_proj = joined[:, :, rank:]
    train_grads = jnp.einsum(
        "esi,esj->eij",
        in_proj,
        out_proj,
        precision=lax.Precision.HIGHEST,
        preferred_element_type=jnp.float32,
    ).reshape(e_dev, rank * rank)
    squares = lax.psum(jnp.sum(train_grads * train_grads, axis=0), "dp")
    moment = squares / (e_dev * lax.axis_size("dp"))
    precond = 1.0 / (moment + 0.1 * jnp.mean(moment))
    weighted = train_grads * precond[None, :]
    return (
        jnp.dot(
            weighted,
            lax.all_gather(query_grads, "dp", axis=0, tiled=True).T,
            precision=lax.Precision.HIGHEST,
            preferred_element_type=jnp.float32,
        )
        / rank
    )


def solution(mesh):
    in_specs = (
        P("dp", None, "tensor"),
        P("dp", None, "tensor"),
        P("dp", None, "tensor"),
        P("dp"),
        P("tensor", None),
        P("tensor", None),
        P("dp", None),
    )
    out_specs = P("dp", None)
    return jax.shard_map(
        per_device, mesh=mesh, in_specs=in_specs, out_specs=out_specs, check_vma=False
    )
```

profile of v0, /device:TPU:0, one launch (start us, length us, event | category | flops | bytes accessed | tf_op | source)
XLA Modules:
  0.0 100.0 jit_solution(14919817355727266009)
XLA Ops:
  7.4 0.0 copy-start
  7.4 0.0 all-reduce.2.cloned.1.call-start
  7.4 1.2 %copy-done = bf16[4,64,2048]{2,1,0:T(8,128)(2,1)S(1)} copy-done((bf16[4,64,2048]{2,1,0:T(8,128)(2,1)S(1)}, bf16[4,64,2048]{2,1,0:T(8,128)(2,1)}, u32[]{:S(2)}) %copy-start) | copy-done | bytes 1048600
  8.6 1.4 %fusion.8 = f32[4,64,64]{2,1,0:T(8,128)S(1)} fusion(bf16[4,64,2048]{2,1,0:T(8,128)(2,1)S(1)} %copy-done, bf16[2048,64]{0,1:T(8,128)(2,1)} %param.12), kind=kOutput, calls=%fused_computation.10 | convolution fusion | flops 67108864 | bytes 1376256 | tf_op jit(solution)/shard_map/esd,dr->esr/dot_general | solution.py:15
  10.0 0.0 copy-start.1
  10.0 4.7 %fusion.5 = f32[4,64,64]{2,1,0:T(8,128)S(1)} fusion(bf16[4,64,7168]{2,1,0:T(8,128)(2,1)} %param.8, bf16[4,64,7168]{2,1,0:T(8,128)(2,1)} %param.7, bf16[7168,64]{0,1:T(8,128)(2,1)} %param.11), kind=kOutput, calls=%fused_computation.7 | convolution fusion | flops 249561088 | bytes 8323072 | tf_op jit(solution)/shard_map/esf,fr->esr/dot_general | solution.py:14
  14.7 0.8 pad_maximum_fusion
  15.4 0.0 all-reduce.2.cloned.1.call-update
  15.5 0.0 all-gather.2.cloned.1.call-start
  15.5 0.5 all-gather.2.cloned.1.call-update
  16.0 0.0 copy-done.1
  16.1 0.1 fusion.15
  16.1 33.6 %all-reduce.2.cloned.1.call-done = f32[4,64,128]{2,1,0:T(8,128)} async-done(((f32[4,64,128]{2,1,0:T(8,128)}), f32[4,64,128]{2,1,0:T(8,128)}) %all-reduce.2.cloned.1.call-update) | async-done | bytes 131088 | tf_op jit(solution)/shard_map/psum | solution.py:16
  49.8 1.5 %multiply_reduce_fusion = (f32[64,64]{1,0:T(8,128)S(1)}, f32[4,64,64]{2,1,0:T(8,128)S(1)}) fusion(f32[4,64,128]{2,1,0:T(8,128)} %all-reduce.2.cloned.1.call-done, f32[4,64]{1,0:T(4,128)S(1)} %fusion.15), kind=kOutput, calls=%fused_computation.16 | convolution fusion | flops 12627968 | bytes 345088 | tf_op jit(solution)/shard_map/esi,esj->eij/dot_general | solution.py:20
  51.2 0.1 reduce_sum.21
  51.3 0.1 reshape.27
  51.4 37.1 %psum.15 = f32[4096]{0:T(1024)S(1)} all-reduce(f32[4096]{0:T(1024)S(1)} %reduce_sum.21), channel_id=1, replica_groups=mesh['dp'=8,'tensor'=4] {'dp'}, use_global_device_ids=true, to_apply=%region_2.3 | all-reduce | flops 4096 | bytes 32768 | tf_op jit(solution)/shard_map/psum | solution.py:27
  88.5 0.6 multiply_reduce_fusion.1
  89.8 0.0 all-gather.2.cloned.1.call-done
  89.8 2.7 %convolution_multiply_fusion = f32[4,64]{1,0:T(4,128)} fusion(f32[64,4096]{1,0:T(8,128)} %all-gather.2.cloned.1.call-done, f32[4,4096]{1,0:T(4,128)S(1)} %reshape.27, f32[4096]{0:T(1024)S(1)} %add_divide_fusion), kind=kOutput, calls=%fused_computation.8 | convolution fusion | flops 12599552 | bytes 1131520 | tf_op jit(solution)/shard_map/dot_general | solution.py:32
  (1 shorter events, 0.0 us)
Async XLA Ops:
  7.4 1.2 %copy-start = (bf16[4,64,2048]{2,1,0:T(8,128)(2,1)S(1)}, bf16[4,64,2048]{2,1,0:T(8,128)(2,1)}, u32[]{:S(2)}) copy-start(bf16[4,64,2048]{2,1,0:T(8,128)(2,1)} %param.9) | copy-start | bytes 3145732
  7.4 42.4 %all-reduce.2.cloned.1.call-start = ((), (), s32[]{:S(2)}) async-start(), calls=%async_computation | async-start | bytes 262144 | tf_op jit(solution)/shard_map/psum | solution.py:16
  10.0 6.1 %copy-start.1 = (s32[4]{0:T(128)S(1)}, s32[4]{0:T(128)}, u32[]{:S(2)}) copy-start(s32[4]{0:T(128)} %param.10) | copy-start | bytes 52
  15.5 74.3 %all-gather.2.cloned.1.call-start = ((), (), s32[]{:S(2)}) async-start(), calls=%async_computation.1 | async-start | bytes 1179648 | tf_op jit(solution)/shard_map/all_gather | solution.py:34
Sparse Core Ops, SparseCore 0:
  15.6 34.1 all-reduce.1
Sparse Core Ops, SparseCore 1:
  18.1 43.1 all-gather.1
where the time goes:
time: 100 us
  blocking collectives  37.1 us (37%)
  waiting for transfers between devices  34.2 us (34%)
  between operations  15.5 us (16%)
  matrix products  10.2 us (10%)
  other arithmetic  1.44 us (1%)
  local copies, waits for them, and re-layouts  1.41 us (1%)
    psum x1, blocking collectives, per_device(): squares = lax.psum(jnp.sum(train_grads * train_grads, axis=0), 'dp')  37.1 us
    psum x1, waiting for transfers between devices, per_device(): joined = lax.psum(jnp.concatenate([in_part, out_part], axis=2), 'tensor')  33.6 us
    dot_general x1, matrix products, per_device(): jnp.einsum('esf,fr->esr', hidden, proj_hidden, preferred_element_type=jnp...  4.69 us
    dot_general x1, matrix products, per_device(): jnp.dot(weighted, lax.all_gather(query_grads, 'dp', axis=0, tiled=True).T...  2.73 us
  transfers between devices with their start and end apart: 2, of which 1 were waited for; matrix products, arithmetic and copies ran while one was open for 2% of the time, Pallas kernels for 0%

commit v1 on v0

v1 whole, which is shorter than its diff:
```python
import functools

import jax
import jax.numpy as jnp
from jax import lax
from jax.experimental import pallas as pl
from jax.experimental.pallas import tpu as pltpu
from jax.sharding import PartitionSpec as P

MESH = pl.DeviceIdType.MESH
LANES = 128
DAMPING = 0.1


def contract_last(a, b, precision=None):
    return lax.dot_general(
        a, b, (((1,), (1,)), ((), ())), precision=precision, preferred_element_type=jnp.float32
    )


def pieces(size, most):
    count = -(-size // most)
    while size % (count * LANES):
        count += 1
    return count, size // count


def kernel(
    ndp,
    nt,
    length_ref,
    gate_hbm,
    up_hbm,
    grad_hbm,
    wh_hbm,
    wo_hbm,
    query_hbm,
    out_ref,
    gate,
    up,
    grad,
    wh,
    wo,
    queries,
    send1,
    recv1,
    tg_ref,
    send2,
    recv2,
    send3,
    recv3,
    gate_sem,
    up_sem,
    grad_sem,
    wh_sem,
    wo_sem,
    query_sem,
    query_send,
    query_recv,
    send1_sem,
    recv1_sem,
    send2_sem,
    recv2_sem,
    send3_sem,
    recv3_sem,
):
    seq = gate.shape[1]
    rank = wh.shape[0]
    halves, half = gate_sem.shape[1], gate.shape[2] // gate_sem.shape[1]
    feats = grad.shape[2]
    slices = rank * rank // LANES
    group = slices // nt
    ndev = ndp * nt
    nq = queries.shape[0] * queries.shape[1]
    pack = max(1, LANES // nq)
    per_row = nt // pack

    dp = lax.axis_index("dp")
    t = lax.axis_index("tensor")
    me = dp * nt + t

    def slice_of(d, x):
        return lax.rem(d, group) * nt + x

    def slot_of(d, x):
        g, local = d // group, lax.rem(d, group)
        return g * slices + lax.rem(x, pack) * (slices // pack) + local * per_row + x // pack

    def peer(i):
        p = lax.rem(me + i, ndev)
        return p // nt, lax.rem(p, nt)

    def example(s):
        return lax.rem(t + 1 + s, nt)

    barrier = pltpu.get_barrier_semaphore()

    def greet(i, c):
        pl.semaphore_signal(barrier, inc=1, device_id=peer(i), device_id_type=MESH)
        return c

    def gate_copy(e, h):
        cols = pl.ds(h * half, half)
        return pltpu.make_async_copy(
            gate_hbm.at[e, :, cols], gate.at[e, :, cols], gate_sem.at[e, h]
        )

    def up_copy(e, h):
        cols = pl.ds(h * half, half)
        return pltpu.make_async_copy(up_hbm.at[e, :, cols], up.at[e, :, cols], up_sem.at[e, h])

    def grad_copy(e):
        return pltpu.make_async_copy(grad_hbm.at[e], grad.at[e], grad_sem.at[e])

    def wh_copy(h):
        cols = pl.ds(h * half, half)
        return pltpu.make_async_copy(wh_hbm.at[:, cols], wh.at[:, cols], wh_sem.at[h])

    def query_cols(d):
        return pl.ds(pl.multiple_of(slice_of(d, t) * LANES, LANES), LANES)

    wo_copy = pltpu.make_async_copy(wo_hbm, wo, wo_sem)
    own_query = pltpu.make_async_copy(query_hbm.at[:, query_cols(dp)], queries.at[dp], query_sem)

    wo_copy.start()
    for s in range(nt):
        e = example(s)
        grad_copy(e).start()
        for h in range(halves):
            if s == 0:
                wh_copy(h).start()
            gate_copy(e, h).start()
            up_copy(e, h).start()
    own_query.start()
    lax.fori_loop(1, ndev, greet, 0)
    wo_copy.wait()

    def partial_of(s):
        e = example(s)
        grad_copy(e).wait()
        out_part = contract_last(grad[e], wo[...])
        in_part = jnp.zeros((seq, rank), jnp.float32)
        for h in range(halves):
            if s == 0:
                wh_copy(h).wait()
            gate_copy(e, h).wait()
            up_copy(e, h).wait()
            count, width = pieces(half, 512)
            for c in range(count):
                cols = pl.ds(h * half + c * width, width)
                a = gate[e, :, cols].astype(jnp.float32) * 0.5
                u = up[e, :, cols].astype(jnp.float32)
                hidden = (u * (a + a * jnp.tanh(a))).astype(jnp.bfloat16)
                in_part = in_part + contract_last(hidden, wh[:, cols])
        return jnp.concatenate([in_part, out_part], axis=1)

    def reduce_copy(s):
        return pltpu.make_async_remote_copy(
            send1.at[s],
            recv1.at[s],
            send1_sem.at[s],
            recv1_sem.at[s],
            device_id=(dp, example(s)),
            device_id_type=MESH,
        )

    def query_copy(i):
        d = lax.rem(dp + i, ndp)
        return pltpu.make_async_remote_copy(
            query_hbm.at[:, query_cols(d)],
            queries.at[dp],
            query_send,
            query_recv,
            device_id=(d, t),
            device_id_type=MESH,
        )

    for s in range(nt - 1):
        send1[s] = partial_of(s)
        if s == 0:
            pl.semaphore_wait(barrier, ndev - 1)
        reduce_copy(s).start()
        if s == 0:

            def send_query(i, c):
                query_copy(i).start()
                return c

            lax.fori_loop(1, ndp, send_query, 0)
    joined = partial_of(nt - 1)
    for s in range(nt - 1):
        reduce_copy(s).wait_recv()
        joined = joined + recv1[s]

    rows = lax.broadcasted_iota(jnp.int32, (seq, rank), 0)
    in_proj = jnp.where(rows < length_ref[t], joined[:, :rank], 0.0)
    tg_ref[...] = lax.dot_general(
        in_proj,
        joined[:, rank:],
        (((0,), (0,)), ((), ())),
        precision=lax.Precision.HIGHEST,
        preferred_element_type=jnp.float32,
    )
    per_slice = LANES // rank
    flat = jnp.concatenate(
        [tg_ref[pl.ds(r, slices, stride=per_slice), :] for r in range(per_slice)], axis=1
    )
    norm = jnp.sum(flat * flat, axis=0, keepdims=True)
    send2[:, 0, :] = flat
    send2[:, 1, :] = jnp.broadcast_to(norm, (slices, LANES))

    my_slot = slot_of(dp, t)
    my_slice = slice_of(dp, t)

    def grads_copy(i):
        d, x = peer(i)
        return pltpu.make_async_remote_copy(
            send2.at[slice_of(d, x)],
            recv2.at[my_slot],
            send2_sem,
            recv2_sem,
            device_id=(d, x),
            device_id_type=MESH,
        )

    def send_grads(i, c):
        grads_copy(i).start()
        return c

    lax.fori_loop(1, ndev, send_grads, 0)
    recv2[my_slot] = send2[my_slice]
    own_query.wait()
    others = queries.at[pl.ds(0, ndp - 1)]
    pltpu.make_async_copy(others, others, query_recv).wait()
    others = recv2.at[pl.ds(0, ndev - 1)]
    pltpu.make_async_copy(others, others, recv2_sem).wait()

    everyone = recv2[...]
    examples = ndp * nt
    moment = jnp.sum(everyone * everyone, axis=0)[0:1] / examples
    norms = jnp.sum(everyone, axis=0)[1:2]
    mean = jnp.sum(norms, axis=1, keepdims=True) / (examples * rank * rank)
    precond = 1.0 / (moment + DAMPING * mean)
    first = pl.multiple_of((dp // group) * slices, slices)
    grads = recv2[pl.ds(first, slices), 0, :]
    scores = contract_last(
        grads * precond, queries[...].reshape(nq, LANES), precision=lax.Precision.HIGHEST
    )
    block = slices // pack
    packed = jnp.concatenate([scores[r * block : (r + 1) * block] for r in range(pack)], axis=1)
    for d in range(group):
        send3[d] = packed[d * per_row : (d + 1) * per_row]

    my_group = dp // group

    def scores_copy(i):
        p = lax.rem(my_slice + i, slices)
        d, x = p // nt, lax.rem(p, nt)
        return pltpu.make_async_remote_copy(
            send3.at[d],
            recv3.at[my_slice],
            send3_sem,
            recv3_sem,
            device_id=(my_group * group + d, x),
            device_id_type=MESH,
        )

    def send_scores(i, c):
        scores_copy(i).start()
        return c

    lax.fori_loop(1, slices, send_scores, 0)
    recv3[my_slice] = send3[lax.rem(dp, group)]
    others = recv3.at[pl.ds(0, slices - 1)]
    pltpu.make_async_copy(others, others, recv3_sem).wait()
    total = jnp.sum(recv3[...], axis=0) * (1.0 / rank)
    for r in range(per_row):
        for c in range(pack):
            row = r * pack + c
            out_ref[row : row + 1, :] = total[r : r + 1, c * nq : (c + 1) * nq]

    for s in range(nt - 1):
        reduce_copy(s).wait_send()
    others = queries.at[pl.ds(0, ndp - 1)]
    pltpu.make_async_copy(others, others, query_send).wait()
    others = recv2.at[pl.ds(0, ndev - 1)]
    pltpu.make_async_copy(others, others, send2_sem).wait()
    others = recv3.at[pl.ds(0, slices - 1)]
    pltpu.make_async_copy(others, others, send3_sem).wait()


def per_device(
    ndp, nt, gate_pre, up_pre, out_grad, lengths, proj_hidden, proj_out, query_grads
):
    e_dev, seq, ff = gate_pre.shape
    feats = out_grad.shape[2]
    rank = proj_hidden.shape[1]
    q_dev = query_grads.shape[0]
    nq = q_dev * ndp
    slices = rank * rank // LANES
    group = slices // nt
    assert e_dev == nt and slices % nt == 0 and ndp % group == 0
    pack = max(1, LANES // nq)
    per_row = nt // pack
    halves = 2
    f32, bf16 = jnp.float32, jnp.bfloat16
    dma = pltpu.SemaphoreType.DMA
    anywhere = pl.BlockSpec(memory_space=pl.ANY)
    return pl.pallas_call(
        functools.partial(kernel, ndp, nt),
        out_shape=jax.ShapeDtypeStruct((e_dev, nq), f32),
        in_specs=[pl.BlockSpec(memory_space=pltpu.SMEM)] + [anywhere] * 6,
        out_specs=pl.BlockSpec(memory_space=pltpu.VMEM),
        scratch_shapes=[
            pltpu.VMEM((e_dev, seq, ff), bf16),
            pltpu.VMEM((e_dev, seq, ff), bf16),
            pltpu.VMEM((e_dev, seq, feats), bf16),
            pltpu.VMEM((rank, ff), bf16),
            pltpu.VMEM((rank, feats), bf16),
            pltpu.VMEM((ndp, q_dev, LANES), f32),
            pltpu.VMEM((nt - 1, seq, 2 * rank), f32),
            pltpu.VMEM((nt - 1, seq, 2 * rank), f32),
            pltpu.VMEM((rank, rank), f32),
            pltpu.VMEM((slices, 2, LANES), f32),
            pltpu.VMEM((ndp * nt, 2, LANES), f32),
            pltpu.VMEM((group, per_row, pack * nq), f32),
            pltpu.VMEM((slices, per_row, pack * nq), f32),
            dma((e_dev, halves)),
            dma((e_dev, halves)),
            dma((e_dev,)),
            dma((halves,)),
            dma,
            dma,
            dma,
            dma,
            dma((nt - 1,)),
            dma((nt - 1,)),
            dma,
            dma,
            dma,
            dma,
        ],
        compiler_params=pltpu.CompilerParams(
            collective_id=0, has_side_effects=True, vmem_limit_bytes=48 * 1024 * 1024
        ),
        cost_estimate=pl.CostEstimate(
            flops=2 * e_dev * seq * (ff + feats) * rank,
            bytes_accessed=4 * e_dev * seq * ff + 2 * e_dev * seq * feats,
            transcendentals=e_dev * seq * ff,
        ),
    )(lengths, gate_pre, up_pre, out_grad, proj_hidden.T, proj_out.T, query_grads)


def solution(mesh):
    in_specs = (
        P("dp", None, "tensor"),
        P("dp", None, "tensor"),
        P("dp", None, "tensor"),
        P("dp"),
        P("tensor", None),
        P("tensor", None),
        P("dp", None),
    )
    return jax.shard_map(
        functools.partial(per_device, mesh.shape["dp"], mesh.shape["tensor"]),
        mesh=mesh,
        in_specs=in_specs,
        out_specs=P("dp", None),
        check_vma=False,
    )
```

time: 100 us -> 30 us (0.30)
  blocking collectives: 37.1 us -> 0 us
  waiting for transfers between devices: 34.2 us -> 0 us
  Pallas kernels: 0 us -> 22.1 us
  between operations: 15.5 us -> 0.02 us
  matrix products: 10.2 us -> 0 us
  local copies, waits for them, and re-layouts: 1.41 us -> 7.53 us
  other arithmetic: 1.44 us -> 0 us
    psum x1 -> x0, blocking collectives: 37.1 us -> none  [per_device(): squares = lax.psum(jnp.sum(train_grads * train_grads, axis=0), 'dp')]
    psum x1 -> x0, waiting for transfers between devices: 33.6 us -> none  [per_device(): joined = lax.psum(jnp.concatenate([in_part, out_part], axis=2), 'tensor')]
    pallas_call x0 -> x1, Pallas kernels: none -> 22.1 us  [per_device(): pl.pallas_call(functools.partial(kernel, ndp, nt), out_shape=jax.ShapeDty...]
    dot_general x4 -> x0, matrix products: 10.2 us -> none  [the longest x1 4.69 us: per_device(): jnp.einsum('esf,fr->esr', hidden, proj_hidden, preferred_element_type=jnp...]
    unnamed x4 -> x13, local copies, waits for them, and re-layouts: 1.23 us -> 7.53 us
  transfers between devices with their start and end apart: 2 -> 0, of which waited for: 1 -> 0; matrix products, arithmetic and copies ran while one was open for 2% -> 0% of each run, Pallas kernels for 0% -> 0%
where the time goes in v1:
time: 30 us; the launch traced here: 29.7 us
  Pallas kernels  22.1 us (74%)
  local copies, waits for them, and re-layouts  7.53 us (25%)
    pallas_call x1, Pallas kernels, per_device(): pl.pallas_call(functools.partial(kernel, ndp, nt), out_shape=jax.ShapeDty...  22.1 us
    unnamed x13, local copies, waits for them, and re-layouts  7.53 us

profile of v1, /device:TPU:0, one launch (start us, length us, event | category | flops | bytes accessed | tf_op | source)
XLA Modules:
  0.0 29.7 jit_solution(12883176593975589553)
XLA Ops:
  0.0 0.0 copy-start
  0.0 2.0 %copy-done = bf16[4,64,7168]{2,1,0:T(8,128)(2,1)S(1)} copy-done((bf16[4,64,7168]{2,1,0:T(8,128)(2,1)S(1)}, bf16[4,64,7168]{2,1,0:T(8,128)(2,1)}, u32[]{:S(2)}) %copy-start) | copy-done | bytes 3670040
  2.0 0.0 copy-start.1
  2.0 1.2 %copy-done.1 = bf16[4,64,2048]{2,1,0:T(8,128)(2,1)S(1)} copy-done((bf16[4,64,2048]{2,1,0:T(8,128)(2,1)S(1)}, bf16[4,64,2048]{2,1,0:T(8,128)(2,1)}, u32[]{:S(2)}) %copy-start.1) | copy-done | bytes 1048600
  3.3 0.0 copy-start.2
  3.3 1.2 %copy-done.2 = bf16[7168,64]{0,1:T(8,128)(2,1)S(1)} copy-done((bf16[7168,64]{0,1:T(8,128)(2,1)S(1)}, bf16[7168,64]{0,1:T(8,128)(2,1)}, u32[]{:S(2)}) %copy-start.2) | copy-done | bytes 917528
  4.4 0.0 copy-start.3
  4.4 0.9 %copy-done.3 = bf16[2048,64]{0,1:T(8,128)(2,1)S(1)} copy-done((bf16[2048,64]{0,1:T(8,128)(2,1)S(1)}, bf16[2048,64]{0,1:T(8,128)(2,1)}, u32[]{:S(2)}) %copy-start.3) | copy-done | bytes 262168
  5.4 0.0 copy-start.4
  5.4 0.9 %copy-done.4 = f32[8,4096]{1,0:T(8,128)S(1)} copy-done((f32[8,4096]{1,0:T(8,128)S(1)}, f32[8,4096]{1,0:T(8,128)}, u32[]{:S(2)}) %copy-start.4) | copy-done | bytes 131096
  6.3 0.0 copy-start.5
  6.3 0.7 %copy-done.5 = s32[4]{0:T(128)S(1)} copy-done((s32[4]{0:T(128)S(1)}, s32[4]{0:T(128)}, u32[]{:S(2)}) %copy-start.5) | copy-done | bytes 40
  7.0 22.1 %shard_map.73 = f32[4,64]{1,0:T(4,128)S(1)} custom-call(s32[4]{0:T(128)S(1)} %copy-done.5, bf16[4,64,7168]{2,1,0:T(8,128)(2,1)S(1)} %copy-done, bf16[4,64,7168]{2,1,0:T(8,128)(2,1)} %up_hbm.1, bf16[4,64,2048]{2,1,0:T(8,128)(2,1)S(1)} %copy-done.1, bf16[64,7168]{1,0:T(8,128)(2,1)S(1)} %bitcast.2, bf16[64,2048]{1,0:T(8,128)(2,1)S(1)} %bitcast.3, ...), custom_call_target="tpu_custom_call" | custom-call | flops 301989888 | bytes 8388608 | tf_op jit(solution)/shard_map/pallas_call | solution.py:309
  29.1 0.6 %copy.9 = f32[4,64]{1,0:T(4,128)} copy(f32[4,64]{1,0:T(4,128)S(1)} %shard_map.73) | data formatting | bytes 2048
Async XLA Ops:
  0.0 2.0 %copy-start = (bf16[4,64,7168]{2,1,0:T(8,128)(2,1)S(1)}, bf16[4,64,7168]{2,1,0:T(8,128)(2,1)}, u32[]{:S(2)}) copy-start(bf16[4,64,7168]{2,1,0:T(8,128)(2,1)} %gate_hbm.1) | copy-start | bytes 11010052
  2.0 1.2 %copy-start.1 = (bf16[4,64,2048]{2,1,0:T(8,128)(2,1)S(1)}, bf16[4,64,2048]{2,1,0:T(8,128)(2,1)}, u32[]{:S(2)}) copy-start(bf16[4,64,2048]{2,1,0:T(8,128)(2,1)} %grad_hbm.1) | copy-start | bytes 3145732
  3.3 1.2 %copy-start.2 = (bf16[7168,64]{0,1:T(8,128)(2,1)S(1)}, bf16[7168,64]{0,1:T(8,128)(2,1)}, u32[]{:S(2)}) copy-start(bf16[7168,64]{0,1:T(8,128)(2,1)} %param.11) | copy-start | bytes 2752516
  4.4 0.9 %copy-start.3 = (bf16[2048,64]{0,1:T(8,128)(2,1)S(1)}, bf16[2048,64]{0,1:T(8,128)(2,1)}, u32[]{:S(2)}) copy-start(bf16[2048,64]{0,1:T(8,128)(2,1)} %param.12) | copy-start | bytes 786436
  5.4 0.9 %copy-start.4 = (f32[8,4096]{1,0:T(8,128)S(1)}, f32[8,4096]{1,0:T(8,128)}, u32[]{:S(2)}) copy-start(f32[8,4096]{1,0:T(8,128)} %query_hbm.1) | copy-start | bytes 393220
  6.3 0.7 %copy-start.5 = (s32[4]{0:T(128)S(1)}, s32[4]{0:T(128)}, u32[]{:S(2)}) copy-start(s32[4]{0:T(128)} %length_ref.1) | copy-start | bytes 52

commit v2 on v1

--- a/solution.py
+++ b/solution.py
@@ -28,7 +28,7 @@
 def kernel(
     ndp,
     nt,
-    length_ref,
+    length_hbm,
     gate_hbm,
     up_hbm,
     grad_hbm,
@@ -36,6 +36,7 @@
     wo_hbm,
     query_hbm,
     out_ref,
+    length_ref,
     gate,
     up,
     grad,
@@ -49,6 +50,7 @@
     recv2,
     send3,
     recv3,
+    length_sem,
     gate_sem,
     up_sem,
     grad_sem,
@@ -119,6 +121,7 @@
     def query_cols(d):
         return pl.ds(pl.multiple_of(slice_of(d, t) * LANES, LANES), LANES)
 
+    length_copy = pltpu.make_async_copy(length_hbm, length_ref, length_sem)
     wo_copy = pltpu.make_async_copy(wo_hbm, wo, wo_sem)
     own_query = pltpu.make_async_copy(query_hbm.at[:, query_cols(dp)], queries.at[dp], query_sem)
 
@@ -132,6 +135,7 @@
             gate_copy(e, h).start()
             up_copy(e, h).start()
     own_query.start()
+    length_copy.start()
     lax.fori_loop(1, ndev, greet, 0)
     wo_copy.wait()
 
@@ -192,6 +196,7 @@
         reduce_copy(s).wait_recv()
         joined = joined + recv1[s]
 
+    length_copy.wait()
     rows = lax.broadcasted_iota(jnp.int32, (seq, rank), 0)
     in_proj = jnp.where(rows < length_ref[t], joined[:, :rank], 0.0)
     tg_ref[...] = lax.dot_general(
@@ -305,13 +310,14 @@
     halves = 2
     f32, bf16 = jnp.float32, jnp.bfloat16
     dma = pltpu.SemaphoreType.DMA
-    anywhere = pl.BlockSpec(memory_space=pl.ANY)
+    in_hbm = pl.BlockSpec(memory_space=pl.ANY)
     return pl.pallas_call(
         functools.partial(kernel, ndp, nt),
         out_shape=jax.ShapeDtypeStruct((e_dev, nq), f32),
-        in_specs=[pl.BlockSpec(memory_space=pltpu.SMEM)] + [anywhere] * 6,
+        in_specs=[in_hbm] * 7,
         out_specs=pl.BlockSpec(memory_space=pltpu.VMEM),
         scratch_shapes=[
+            pltpu.SMEM((e_dev,), jnp.int32),
             pltpu.VMEM((e_dev, seq, ff), bf16),
             pltpu.VMEM((e_dev, seq, ff), bf16),
             pltpu.VMEM((e_dev, seq, feats), bf16),
@@ -325,6 +331,7 @@
             pltpu.VMEM((ndp * nt, 2, LANES), f32),
             pltpu.VMEM((group, per_row, pack * nq), f32),
             pltpu.VMEM((slices, per_row, pack * nq), f32),
+            dma,
             dma((e_dev, halves)),
             dma((e_dev, halves)),
             dma((e_dev,)),
@@ -341,7 +348,7 @@
             dma,
         ],
         compiler_params=pltpu.CompilerParams(
-            collective_id=0, has_side_effects=True, vmem_limit_bytes=48 * 1024 * 1024
+            collective_id=0, has_side_effects=True, vmem_limit_bytes=64 * 1024 * 1024
         ),
         cost_estimate=pl.CostEstimate(
             flops=2 * e_dev * seq * (ff + feats) * rank,

time: 30 us -> 23.3 us (0.78)
  local copies, waits for them, and re-layouts: 7.53 us -> 1.26 us
    unnamed x13 -> x1, local copies, waits for them, and re-layouts: 7.53 us -> 1.26 us
where the time goes in v2:
time: 23.3 us; the launch traced here: 23.1 us
  Pallas kernels  21.9 us (94%)
  local copies, waits for them, and re-layouts  1.26 us (5%)
    pallas_call x1, Pallas kernels, per_device(): pl.pallas_call(functools.partial(kernel, ndp, nt), out_shape=jax.ShapeDty...  21.9 us
    unnamed x1, local copies, waits for them, and re-layouts  1.26 us

profile of v2, /device:TPU:0, one launch (start us, length us, event | category | flops | bytes accessed | tf_op | source)
XLA Modules:
  0.0 23.1 jit_solution(12573350128550390543)
XLA Ops:
  0.0 21.9 %shard_map.73 = f32[4,64]{1,0:T(4,128)} custom-call(s32[4]{0:T(128)} %length_hbm.1, bf16[4,64,7168]{2,1,0:T(8,128)(2,1)} %gate_hbm.1, bf16[4,64,7168]{2,1,0:T(8,128)(2,1)} %up_hbm.1, bf16[4,64,2048]{2,1,0:T(8,128)(2,1)} %grad_hbm.1, bf16[64,7168]{1,0:T(8,128)(2,1)} %bitcast.2, bf16[64,2048]{1,0:T(8,128)(2,1)} %bitcast.3, f32[8,4096]{1,0:T(8,128)} %query_hbm.1), custom_call_target="tpu_custom_call" | custom-call | flops 301989888 | bytes 8388608 | tf_op jit(solution)/shard_map/pallas_call | solution.py:314
  21.9 1.3 %copy.9 = f32[4,64]{1,0:T(4,128)} copy(f32[4,64]{1,0:T(4,128)} %shard_map.73) | data formatting | bytes 2048

commit v3 on v2

--- a/solution.py
+++ b/solution.py
@@ -12,10 +12,39 @@
 DAMPING = 0.1
 
 
-def contract_last(a, b, precision=None):
+def contract_last(a, b):
     return lax.dot_general(
-        a, b, (((1,), (1,)), ((), ())), precision=precision, preferred_element_type=jnp.float32
-    )
+        a, b, (((1,), (1,)), ((), ())), preferred_element_type=jnp.float32
+    )
+
+
+def high_low(v):
+    high = v.astype(jnp.bfloat16)
+    return high, (v - high.astype(jnp.float32)).astype(jnp.bfloat16)
+
+
+def left_terms(v, axis):
+    high, low = high_low(v)
+    return jnp.concatenate([high, high, low], axis=axis)
+
+
+def right_terms(v, axis):
+    high, low = high_low(v)
+    return jnp.concatenate([high, low, high], axis=axis)
+
+
+def each(count, body, block=8):
+    full = count // block
+
+    def several(b, c):
+        for j in range(block):
+            body(1 + b * block + j)
+        return c
+
+    if full:
+        lax.fori_loop(0, full, several, 0)
+    for j in range(full * block, count):
+        body(1 + j)
 
 
 def pieces(size, most):
@@ -81,25 +110,28 @@
     t = lax.axis_index("tensor")
     me = dp * nt + t
 
+    def within(d):
+        return d if group == ndp else lax.rem(d, group)
+
     def slice_of(d, x):
-        return lax.rem(d, group) * nt + x
+        return within(d) * nt + x
 
     def slot_of(d, x):
-        g, local = d // group, lax.rem(d, group)
-        return g * slices + lax.rem(x, pack) * (slices // pack) + local * per_row + x // pack
+        g, local = lax.div(d, group), within(d)
+        place = lax.rem(x, pack) * (slices // pack) + local * per_row + lax.div(x, pack)
+        return g * slices + place
 
     def peer(i):
         p = lax.rem(me + i, ndev)
-        return p // nt, lax.rem(p, nt)
+        return lax.div(p, nt), lax.rem(p, nt)
 
     def example(s):
         return lax.rem(t + 1 + s, nt)
 
     barrier = pltpu.get_barrier_semaphore()
 
-    def greet(i, c):
+    def greet(i):
         pl.semaphore_signal(barrier, inc=1, device_id=peer(i), device_id_type=MESH)
-        return c
 
     def gate_copy(e, h):
         cols = pl.ds(h * half, half)
@@ -136,7 +168,7 @@
             up_copy(e, h).start()
     own_query.start()
     length_copy.start()
-    lax.fori_loop(1, ndev, greet, 0)
+    each(ndev - 1, greet)
     wo_copy.wait()
 
     def partial_of(s):
@@ -185,12 +217,7 @@
             pl.semaphore_wait(barrier, ndev - 1)
         reduce_copy(s).start()
         if s == 0:
-
-            def send_query(i, c):
-                query_copy(i).start()
-                return c
-
-            lax.fori_loop(1, ndp, send_query, 0)
+            each(ndp - 1, lambda i: query_copy(i).start())
     joined = partial_of(nt - 1)
     for s in range(nt - 1):
         reduce_copy(s).wait_recv()
@@ -200,10 +227,9 @@
     rows = lax.broadcasted_iota(jnp.int32, (seq, rank), 0)
     in_proj = jnp.where(rows < length_ref[t], joined[:, :rank], 0.0)
     tg_ref[...] = lax.dot_general(
-        in_proj,
-        joined[:, rank:],
+        left_terms(in_proj, 0),
+        right_terms(joined[:, rank:], 0),
         (((0,), (0,)), ((), ())),
-        precision=lax.Precision.HIGHEST,
         preferred_element_type=jnp.float32,
     )
     per_slice = LANES // rank
@@ -228,15 +254,12 @@
             device_id_type=MESH,
         )
 
-    def send_grads(i, c):
-        grads_copy(i).start()
-        return c
-
-    lax.fori_loop(1, ndev, send_grads, 0)
+    each(ndev - 1, lambda i: grads_copy(i).start())
     recv2[my_slot] = send2[my_slice]
     own_query.wait()
     others = queries.at[pl.ds(0, ndp - 1)]
     pltpu.make_async_copy(others, others, query_recv).wait()
+    query_terms = right_terms(queries[...].reshape(nq, LANES), 1)
     others = recv2.at[pl.ds(0, ndev - 1)]
     pltpu.make_async_copy(others, others, recv2_sem).wait()
 
@@ -246,21 +269,19 @@
     norms = jnp.sum(everyone, axis=0)[1:2]
     mean = jnp.sum(norms, axis=1, keepdims=True) / (examples * rank * rank)
     precond = 1.0 / (moment + DAMPING * mean)
-    first = pl.multiple_of((dp // group) * slices, slices)
+    first = pl.multiple_of(lax.div(dp, group) * slices, slices)
     grads = recv2[pl.ds(first, slices), 0, :]
-    scores = contract_last(
-        grads * precond, queries[...].reshape(nq, LANES), precision=lax.Precision.HIGHEST
-    )
+    scores = contract_last(left_terms(grads * precond, 1), query_terms)
     block = slices // pack
     packed = jnp.concatenate([scores[r * block : (r + 1) * block] for r in range(pack)], axis=1)
     for d in range(group):
         send3[d] = packed[d * per_row : (d + 1) * per_row]
 
-    my_group = dp // group
+    my_group = lax.div(dp, group)
 
     def scores_copy(i):
         p = lax.rem(my_slice + i, slices)
-        d, x = p // nt, lax.rem(p, nt)
+        d, x = lax.div(p, nt), lax.rem(p, nt)
         return pltpu.make_async_remote_copy(
             send3.at[d],
             recv3.at[my_slice],
@@ -270,12 +291,8 @@
             device_id_type=MESH,
         )
 
-    def send_scores(i, c):
-        scores_copy(i).start()
-        return c
-
-    lax.fori_loop(1, slices, send_scores, 0)
-    recv3[my_slice] = send3[lax.rem(dp, group)]
+    each(slices - 1, lambda i: scores_copy(i).start())
+    recv3[my_slice] = send3[within(dp)]
     others = recv3.at[pl.ds(0, slices - 1)]
     pltpu.make_async_copy(others, others, recv3_sem).wait()
     total = jnp.sum(recv3[...], axis=0) * (1.0 / rank)

time: 23.3 us -> 22.8 us (0.979)
  Pallas kernels: 21.9 us -> 21.3 us
    pallas_call x1, Pallas kernels: 21.9 us -> 21.3 us  [per_device(): pl.pallas_call(functools.partial(kernel, ndp, nt), out_shape=jax.ShapeDty...]
where the time goes in v3:
time: 22.8 us; the launch traced here: 22.6 us
  Pallas kernels  21.3 us (93%)
  local copies, waits for them, and re-layouts  1.26 us (6%)
    pallas_call x1, Pallas kernels, per_device(): pl.pallas_call(functools.partial(kernel, ndp, nt), out_shape=jax.ShapeDty...  21.3 us
    unnamed x1, local copies, waits for them, and re-layouts  1.26 us

profile of v3, /device:TPU:0, one launch (start us, length us, event | category | flops | bytes accessed | tf_op | source)
XLA Modules:
  0.0 22.6 jit_solution(1883424520219085440)
XLA Ops:
  0.0 21.3 %shard_map.73 = f32[4,64]{1,0:T(4,128)} custom-call(s32[4]{0:T(128)} %length_hbm.1, bf16[4,64,7168]{2,1,0:T(8,128)(2,1)} %gate_hbm.1, bf16[4,64,7168]{2,1,0:T(8,128)(2,1)} %up_hbm.1, bf16[4,64,2048]{2,1,0:T(8,128)(2,1)} %grad_hbm.1, bf16[64,7168]{1,0:T(8,128)(2,1)} %bitcast.2, bf16[64,2048]{1,0:T(8,128)(2,1)} %bitcast.3, f32[8,4096]{1,0:T(8,128)} %query_hbm.1), custom_call_target="tpu_custom_call" | custom-call | flops 301989888 | bytes 8388608 | tf_op jit(solution)/shard_map/pallas_call | solution.py:331
  21.4 1.3 %copy.9 = f32[4,64]{1,0:T(4,128)} copy(f32[4,64]{1,0:T(4,128)} %shard_map.73) | data formatting | bytes 2048

commit v4 on v3

--- a/solution.py
+++ b/solution.py
@@ -157,6 +157,7 @@
     wo_copy = pltpu.make_async_copy(wo_hbm, wo, wo_sem)
     own_query = pltpu.make_async_copy(query_hbm.at[:, query_cols(dp)], queries.at[dp], query_sem)
 
+    first_sends = min(1, nt - 2)
     wo_copy.start()
     for s in range(nt):
         e = example(s)
@@ -166,9 +167,10 @@
                 wh_copy(h).start()
             gate_copy(e, h).start()
             up_copy(e, h).start()
+        if s == first_sends:
+            each(ndev - 1, greet)
     own_query.start()
     length_copy.start()
-    each(ndev - 1, greet)
     wo_copy.wait()
 
     def partial_of(s):
@@ -213,10 +215,13 @@
 
     for s in range(nt - 1):
         send1[s] = partial_of(s)
-        if s == 0:
+        if s == first_sends:
             pl.semaphore_wait(barrier, ndev - 1)
-        reduce_copy(s).start()
-        if s == 0:
+            for before in range(s):
+                reduce_copy(before).start()
+        if s >= first_sends:
+            reduce_copy(s).start()
+        if s == first_sends:
             each(ndp - 1, lambda i: query_copy(i).start())
     joined = partial_of(nt - 1)
     for s in range(nt - 1):

time: 22.8 us -> 21.9 us (0.961)
  Pallas kernels: 21.3 us -> 20.5 us
    pallas_call x1, Pallas kernels: 21.3 us -> 20.5 us  [per_device(): pl.pallas_call(functools.partial(kernel, ndp, nt), out_shape=jax.ShapeDty...]
where the time goes in v4:
time: 21.9 us; the launch traced here: 21.8 us
  Pallas kernels  20.5 us (94%)
  local copies, waits for them, and re-layouts  1.26 us (6%)
    pallas_call x1, Pallas kernels, per_device(): pl.pallas_call(functools.partial(kernel, ndp, nt), out_shape=jax.ShapeDty...  20.5 us
    unnamed x1, local copies, waits for them, and re-layouts  1.26 us

profile of v4, /device:TPU:0, one launch (start us, length us, event | category | flops | bytes accessed | tf_op | source)
XLA Modules:
  0.0 21.8 jit_solution(15636491187817572255)
XLA Ops:
  0.0 20.5 %shard_map.73 = f32[4,64]{1,0:T(4,128)} custom-call(s32[4]{0:T(128)} %length_hbm.1, bf16[4,64,7168]{2,1,0:T(8,128)(2,1)} %gate_hbm.1, bf16[4,64,7168]{2,1,0:T(8,128)(2,1)} %up_hbm.1, bf16[4,64,2048]{2,1,0:T(8,128)(2,1)} %grad_hbm.1, bf16[64,7168]{1,0:T(8,128)(2,1)} %bitcast.2, bf16[64,2048]{1,0:T(8,128)(2,1)} %bitcast.3, f32[8,4096]{1,0:T(8,128)} %query_hbm.1), custom_call_target="tpu_custom_call" | custom-call | flops 301989888 | bytes 8388608 | tf_op jit(solution)/shard_map/pallas_call | solution.py:336
  20.5 1.3 %copy.9 = f32[4,64]{1,0:T(4,128)} copy(f32[4,64]{1,0:T(4,128)} %shard_map.73) | data formatting | bytes 2048

commit v5 on v4

--- a/solution.py
+++ b/solution.py
@@ -157,7 +157,7 @@
     wo_copy = pltpu.make_async_copy(wo_hbm, wo, wo_sem)
     own_query = pltpu.make_async_copy(query_hbm.at[:, query_cols(dp)], queries.at[dp], query_sem)
 
-    first_sends = min(1, nt - 2)
+    first_sends = nt - 2
     wo_copy.start()
     for s in range(nt):
         e = example(s)
@@ -167,7 +167,7 @@
                 wh_copy(h).start()
             gate_copy(e, h).start()
             up_copy(e, h).start()
-        if s == first_sends:
+        if s == min(1, first_sends):
             each(ndev - 1, greet)
     own_query.start()
     length_copy.start()

time: 21.9 us -> 21.9 us (level)
  no operation moved by 1% of the time
where the time goes in v5:
time: 21.9 us; the launch traced here: 21.7 us
  Pallas kernels  20.5 us (94%)
  local copies, waits for them, and re-layouts  1.26 us (6%)
    pallas_call x1, Pallas kernels, per_device(): pl.pallas_call(functools.partial(kernel, ndp, nt), out_shape=jax.ShapeDty...  20.5 us
    unnamed x1, local copies, waits for them, and re-layouts  1.26 us

profile of v5, /device:TPU:0, one launch (start us, length us, event | category | flops | bytes accessed | tf_op | source)
XLA Modules:
  0.0 21.7 jit_solution(16835376443373864174)
XLA Ops:
  0.0 20.5 %shard_map.73 = f32[4,64]{1,0:T(4,128)} custom-call(s32[4]{0:T(128)} %length_hbm.1, bf16[4,64,7168]{2,1,0:T(8,128)(2,1)} %gate_hbm.1, bf16[4,64,7168]{2,1,0:T(8,128)(2,1)} %up_hbm.1, bf16[4,64,2048]{2,1,0:T(8,128)(2,1)} %grad_hbm.1, bf16[64,7168]{1,0:T(8,128)(2,1)} %bitcast.2, bf16[64,2048]{1,0:T(8,128)(2,1)} %bitcast.3, f32[8,4096]{1,0:T(8,128)} %query_hbm.1), custom_call_target="tpu_custom_call" | custom-call | flops 301989888 | bytes 8388608 | tf_op jit(solution)/shard_map/pallas_call | solution.py:336
  20.5 1.3 %copy.9 = f32[4,64]{1,0:T(4,128)} copy(f32[4,64]{1,0:T(4,128)} %shard_map.73) | data formatting | bytes 2048
